TPU v7x, 256 devices: a whole 4x4x8 slice. The times are simulated.
256 devices in a mesh: rep: 32 (over y, x, core), shard: 8 (over z).
Axes of the slice: x: 4, y: 4, z: 8, core: 2. Of those that a mesh axis runs over, the one named last changes fastest.
Arguments:
- grads: bfloat16 [32, 1024, 8192], P('rep', 'shard'), may hold values from -6 to 6
- errors: bfloat16 [32, 1024, 8192], P('rep', 'shard'), may hold values from -4 to 4
- q_prev: float32 [8192, 128], P('shard'), may hold values from -0.0625 to 0.0625
- moment: float32 [1024, 8192], P('shard'), may hold values from -0.12 to 0.12
- second: float32 [1024, 8192], P('shard'), may hold values from 0.0001 to 0.01
Outputs:
- errors_next: bfloat16 [32, 1024, 8192], P('rep', 'shard')
- q_next: float32 [8192, 128], P('shard')
- moment_next: float32 [1024, 8192], P('shard')
- second_next: float32 [1024, 8192], P('shard')
- update: bfloat16 [1024, 8192], P('shard')
All inputs are finite; a program needn't handle non-finite values.
Results may differ from a plain program's by a relative error of at most 0.0012.
Values sent between devices are 32-bit elements; how exact they have to be, the bound alone decides.
No kernel may reach another device: no remote copies, remote signals or barrier semaphores. Data moves between devices by JAX's collectives and lax.ppermute only.
A program may use at most 128 MiB of HBM per device.

v0:
```python
import jax
import jax.numpy as jnp
from jax import lax
from jax.sharding import PartitionSpec as P

ADAM_STEP = 10


def right_solve(low, values):
    return lax.linalg.triangular_solve(low, values, left_side=False, lower=True, transpose_a=True)


def on_device(grads, errors, q_prev, moment, second):
    hi = lax.Precision.HIGHEST
    q_full = lax.all_gather(q_prev, "shard", axis=0, tiled=True)
    merged = grads[0].astype(jnp.float32) + errors[0].astype(jnp.float32)
    replicas = lax.axis_size("rep")
    p_sum = lax.psum(jnp.dot(merged, q_full, precision=hi), "rep")
    gram_part = jnp.dot(p_sum.T, p_sum, precision=hi)
    gram = lax.psum(gram_part, "shard")
    low = jnp.linalg.cholesky(gram)
    p_hat = right_solve(low, p_sum)
    q_sum = lax.psum(jnp.dot(merged.T, p_hat, precision=hi), ("rep", "shard"))
    q_mean = q_sum / replicas
    approx = jnp.dot(p_hat, q_mean.T, precision=hi)
    errors_next = (merged - approx).astype(jnp.bfloat16)[None]
    width = q_prev.shape[0]
    q_next = lax.dynamic_slice_in_dim(q_mean, lax.axis_index("shard") * width, width, 0)
    moment_next = 0.9 * moment + 0.1 * approx
    second_next = 0.95 * second + 0.05 * approx * approx
    fix_one = 1.0 - 0.9**ADAM_STEP
    fix_two = 1.0 - 0.95**ADAM_STEP
    update = (moment_next / fix_one / (jnp.sqrt(second_next / fix_two) + 1e-08)).astype(
        jnp.bfloat16
    )
    return (errors_next, q_next, moment_next, second_next, update)


def solution(mesh):
    return jax.shard_map(
        on_device,
        mesh=mesh,
        in_specs=(
            P("rep", "shard", None),
            P("rep", "shard", None),
            P("shard", None),
            P("shard", None),
            P("shard", None),
        ),
        out_specs=(
            P("rep", "shard", None),
            P("shard", None),
            P("shard", None),
            P("shard", None),
            P("shard", None),
        ),
        check_vma=False,
    )
```

profile of v0, /device:TPU:1, one launch (start us, length us, event | category | flops | bytes accessed | tf_op | source)
XLA Modules:
  0.0 578.4 jit_solution(9970320081760865877)
XLA Ops:
  7.2 0.0 all-gather.2.cloned.1.call-start
  7.2 0.7 all-gather.2.cloned.1.call-update
  7.9 0.0 copy-start
  7.9 0.0 all-reduce.4.cloned.1.call-start
  8.0 60.5 %all-gather.2.cloned.1.call-done = f32[8192,128]{1,0:T(8,128)} async-done(((f32[1024,128]{1,0:T(8,128)}), f32[8192,128]{1,0:T(8,128)}) %all-gather.2.cloned.1.call-update) | async-done | bytes 4194320 | tf_op jit(solution)/shard_map/all_gather | solution.py:15
  68.4 8.6 %fusion.3 = f32[128,128]{1,0:T(8,128)} fusion(f32[8192,128]{1,0:T(8,128)} %all-gather.2.cloned.1.call-done, bf16[1,128,8192]{2,1,0:T(8,128)(2,1)} %param.6, bf16[1,128,8192]{2,1,0:T(8,128)(2,1)} %param.5), kind=kOutput, calls=%fused_computation.5 | convolution fusion | flops 1613758464 | bytes 8454144 | tf_op jit(solution)/shard_map/dot_general | solution.py:18
  77.0 0.0 all-reduce.4.cloned.1.call-update
  77.0 0.0 all-reduce.6.cloned.1.call-start
  77.1 104.7 %all-reduce.4.cloned.1.call-done = f32[128,128]{1,0:T(8,128)} async-done(((f32[128,128]{1,0:T(8,128)}), f32[128,128]{1,0:T(8,128)}) %all-reduce.4.cloned.1.call-update) | async-done | bytes 65552 | tf_op jit(solution)/shard_map/psum | solution.py:18
  181.8 1.8 fusion.13
  183.6 0.0 all-reduce.6.cloned.1.call-update
  183.7 0.0 all-reduce.8.cloned.1.call-start
  183.7 66.3 %all-reduce.6.cloned.1.call-done = f32[128,128]{0,1:T(8,128)} async-done(((f32[128,128]{0,1:T(8,128)}), f32[128,128]{0,1:T(8,128)}) %all-reduce.6.cloned.1.call-update) | async-done | bytes 65552 | tf_op jit(solution)/shard_map/psum | solution.py:20
  250.0 0.9 copy.11
  250.9 0.9 fusion.10
  251.8 11.7 %cholesky.16 = f32[128,128]{1,0:T(8,128)S(1)} custom-call(f32[128,128]{1,0:T(8,128)S(1)} %fusion.10), custom_call_target="Cholesky" | custom-call | tf_op jit(solution)/shard_map/jit(cholesky)/cholesky | solution.py:21
  263.5 0.6 compare_reduce_fusion
  264.1 0.7 fusion.7
  264.8 9.8 %custom-call.6 = f32[1,128,128]{1,2,0:T(8,128)S(1)} custom-call(f32[1,128,128]{2,1,0:T(8,128)S(1)} %fusion.7), custom_call_target="InvertDiagBlocksLowerTriangular" | custom-call | tf_op jit(solution)/shard_map/triangular_solve | solution.py:10
  274.6 1.0 fusion.8
  275.7 0.0 copy-done
  275.7 9.6 %fusion.1 = f32[8192,128]{1,0:T(8,128)} fusion(f32[128,128]{1,0:T(8,128)S(1)} %fusion.8, bf16[1,128,8192]{2,1,0:T(8,128)(2,1)S(1)} %copy-done, bf16[1,128,8192]{2,1,0:T(8,128)(2,1)} %param.5), kind=kOutput, calls=%fused_computation.3 | convolution fusion | flops 1613758464 | bytes 8454144 | tf_op jit(solution)/shard_map/dot_general | solution.py:23
  285.3 0.0 all-reduce.8.cloned.1.call-update
  285.3 270.5 %all-reduce.8.cloned.1.call-done = f32[8192,128]{1,0:T(8,128)} async-done(((f32[8192,128]{1,0:T(8,128)}), f32[8192,128]{1,0:T(8,128)}) %all-reduce.8.cloned.1.call-update) | async-done | bytes 4194320 | tf_op jit(solution)/shard_map/psum | solution.py:23
  555.9 0.0 copy-start.1
  555.9 0.0 copy-start.2
  555.9 2.6 broadcast_multiply_fusion
  558.5 0.8 constant_dynamic-slice_fusion
  559.3 0.0 copy-done.1
  559.3 0.8 copy-done.2
  560.1 11.7 %divide_convert_fusion = (bf16[128,8192]{1,0:T(8,128)(2,1)}, f32[128,8192]{1,0:T(8,128)}, f32[128,8192]{1,0:T(8,128)}, bf16[1,128,8192]{2,1,0:T(8,128)(2,1)}) fusion(f32[128,8192]{1,0:T(8,128)} %param.9, f32[128,8192]{1,0:T(8,128)} %param.8, bf16[1,128,8192]{2,1,0:T(8,128)(2,1)S(1)} %copy-done, bf16[1,128,8192]{2,1,0:T(8,128)(2,1)S(1)} %copy-done.1, ...), kind=kOutput, calls=%fused_computation.8 | convolution fusion | flops 1629487104 | bytes 29425664 | tf_op jit(solution)/shard_map/dot_general | solution.py:25
  (1 shorter events, 0.0 us)
Async XLA Ops:
  7.2 61.3 %all-gather.2.cloned.1.call-start = ((), (), s32[]{:S(2)}) async-start(), calls=%async_computation | async-start | bytes 4718592 | tf_op jit(solution)/shard_map/all_gather | solution.py:15
  7.9 267.8 %copy-start = (bf16[1,128,8192]{2,1,0:T(8,128)(2,1)S(1)}, bf16[1,128,8192]{2,1,0:T(8,128)(2,1)}, u32[]{:S(2)}) copy-start(bf16[1,128,8192]{2,1,0:T(8,128)(2,1)} %param.6) | copy-start | bytes 6291460
  7.9 173.9 %all-reduce.4.cloned.1.call-start = ((), (), s32[]{:S(2)}) async-start(), calls=%async_computation.1 | async-start | bytes 131072 | tf_op jit(solution)/shard_map/psum | solution.py:18
  77.0 172.9 %all-reduce.6.cloned.1.call-start = ((), (), s32[]{:S(2)}) async-start(), calls=%async_computation.2 | async-start | bytes 131072 | tf_op jit(solution)/shard_map/psum | solution.py:20
  183.7 372.2 %all-reduce.8.cloned.1.call-start = ((), (), s32[]{:S(2)}) async-start(), calls=%async_computation.3 | async-start | bytes 8388608 | tf_op jit(solution)/shard_map/psum | solution.py:23
  555.9 3.5 copy-start.1
  555.9 4.3 copy-start.2
Sparse Core Ops, SparseCore 0:
  9.8 58.6 all-gather.1
  77.2 104.5 all-reduce.3
  184.8 65.1 all-reduce.5
  285.5 270.3 all-reduce.7
where the time goes:
time: 580 us; the launch traced here: 578 us
  waiting for transfers between devices  503 us (87%)
  matrix products  32.8 us (6%)
  other arithmetic  26.3 us (5%)
  between operations  13.8 us (2%)
    psum x1, waiting for transfers between devices, on_device(): q_sum = lax.psum(jnp.dot(merged.T, p_hat, precision=hi), ('rep', 'shard'))  271 us
    psum x1, waiting for transfers between devices, on_device(): p_sum = lax.psum(jnp.dot(merged, q_full, precision=hi), 'rep')  105 us
    psum x1, waiting for transfers between devices, on_device(): gram = lax.psum(gram_part, 'shard')  66.3 us
    all_gather x1, waiting for transfers between devices, on_device(): q_full = lax.all_gather(q_prev, 'shard', axis=0, tiled=True)  60.5 us
    another operation x3, other arithmetic, on_device(): low = jnp.linalg.cholesky(gram)  12.4 us
    dot_general x1, matrix products, on_device(): approx = jnp.dot(p_hat, q_mean.T, precision=hi)  11.7 us
  transfers between devices with their start and end apart: 4, of which 4 were waited for; matrix products, arithmetic and copies ran while one was open for 0% of the time, Pallas kernels for 0%

commit v1 on v0

v1 whole, which is shorter than its diff:
```python
import functools
import math

import jax
import jax.numpy as jnp
from jax import lax
from jax.experimental import pallas as pl
from jax.experimental.pallas import tpu as pltpu
from jax.sharding import Mesh, PartitionSpec as P

ADAM_STEP = 10
HI = lax.Precision.HIGHEST
F32 = jnp.float32
ALL = ("y", "x", "core", "z")
REPS = 32
VMEM_LIMIT = 40 * 1024 * 1024


def vmem():
    return pl.BlockSpec(memory_space=pltpu.VMEM)


def params():
    return pltpu.CompilerParams(vmem_limit_bytes=VMEM_LIMIT)


def dot_nt(a, b):
    return lax.dot_general(a, b, (((1,), (1,)), ((), ())), precision=HI, preferred_element_type=F32)


def add_half(place, grads, errors):
    rows, cols = grads.shape
    wide = cols // 8

    def body(at, g, e, out):
        out[...] = g[...].astype(F32) + e[...].astype(F32)

    half = pl.BlockSpec((rows, wide), lambda i, at: (0, (1 - at[0]) * 4 + i))
    return pl.pallas_call(
        body,
        grid_spec=pltpu.PrefetchScalarGridSpec(
            num_scalar_prefetch=1,
            grid=(4,),
            in_specs=[half, half],
            out_specs=pl.BlockSpec((rows, wide), lambda i, at: (0, i)),
        ),
        out_shape=jax.ShapeDtypeStruct((rows, cols // 2), F32),
        compiler_params=params(),
        name="add_half",
    )(place, grads, errors)


def add_pieces(place, grads, errors, came):
    rows, cols = grads.shape
    wide = cols // 8
    tall = rows // 4

    def body(at, *refs):
        for k in range(4):
            g, e, r = refs[3 * k : 3 * k + 3]
            refs[12 + k][...] = g[...].astype(F32) + e[...].astype(F32) + r[...]

    def own(k):
        return pl.BlockSpec((tall, wide), lambda i, at: (i, at[0] * 4 + (at[1] + k) % 4))

    def other(k):
        return pl.BlockSpec((tall, wide), lambda i, at: (i, (at[1] + k) % 4))

    ins, args = [], []
    for k in range(4):
        ins += [own(k), own(k), other(k)]
        args += [grads, errors, came]
    return pl.pallas_call(
        body,
        grid_spec=pltpu.PrefetchScalarGridSpec(
            num_scalar_prefetch=1,
            grid=(4,),
            in_specs=ins,
            out_specs=[pl.BlockSpec((tall, wide), lambda i, at: (i, 0))] * 4,
        ),
        out_shape=[jax.ShapeDtypeStruct((rows, wide), F32)] * 4,
        compiler_params=params(),
        name="add_pieces",
    )(place, *args)


def sum_split(place, parts):
    rows, cols = parts[0].shape
    wide = cols // 4

    def body(at, *refs):
        for k in range(4):
            block = pl.ds(pl.multiple_of(((at[2] + k) % 4) * wide, wide), wide)
            a, b, c, d = (r[:, block] for r in refs[:4])
            refs[4 + k][...] = (a + b) + (c + d)

    return pl.pallas_call(
        body,
        grid_spec=pltpu.PrefetchScalarGridSpec(
            num_scalar_prefetch=1,
            grid=(1,),
            in_specs=[vmem()] * 4,
            out_specs=[vmem()] * 4,
        ),
        out_shape=[jax.ShapeDtypeStruct((rows, wide), F32)] * 4,
        compiler_params=params(),
        name="sum_split",
    )(place, *parts)


def left_part(parts, right):
    rows, cols = parts[0].shape

    def body(a, b, c, d, q, m_out, p_out):
        m = (a[...] + b[...]) + (c[...] + d[...])
        m_out[...] = m
        p_out[...] = jnp.dot(m, q[...], precision=HI, preferred_element_type=F32)

    return pl.pallas_call(
        body,
        in_specs=[vmem()] * 5,
        out_specs=[vmem()] * 2,
        out_shape=[
            jax.ShapeDtypeStruct((rows, cols), F32),
            jax.ShapeDtypeStruct((rows, right.shape[1]), F32),
        ],
        compiler_params=params(),
        name="left_part",
    )(*parts, right)


def products(m, p):
    cols, rank = m.shape[1], p.shape[1]
    high, low = cols // 8, rank // 8

    def body(m_ref, p_ref, out):
        p_val = p_ref[...]
        t = jnp.dot(m_ref[...].T, p_val, precision=HI, preferred_element_type=F32)
        gram = jnp.dot(p_val.T, p_val, precision=HI, preferred_element_type=F32)
        out[:, :high, :] = t.reshape(8, high, rank)
        out[:, high:, :] = gram.reshape(8, low, rank)

    return pl.pallas_call(
        body,
        in_specs=[vmem()] * 2,
        out_specs=vmem(),
        out_shape=jax.ShapeDtypeStruct((8, high + low, rank), F32),
        compiler_params=params(),
        name="products",
    )(m, p)


def finish(place, which, t, weight, grads, errors, moment, second, before):
    rows, cols = grads.shape
    rank = t.shape[1]
    wide = t.shape[0] // 4
    fix_one = 1.0 / (1.0 - 0.9**ADAM_STEP)
    fix_two = 1.0 / (1.0 - 0.95**ADAM_STEP)
    kc, kx = which

    def body(at, t_ref, w_ref, g, e, m, v, *refs):
        e_out, m_out, v_out, u_out = refs[-4:]
        approx = dot_nt(w_ref[...], t_ref[...])
        merged = g[...].astype(F32) + e[...].astype(F32)
        e_out[...] = (merged - approx).astype(jnp.bfloat16)
        m_next = 0.9 * m[...] + 0.1 * approx
        v_next = 0.95 * v[...] + 0.05 * approx * approx
        m_out[...] = m_next
        v_out[...] = v_next
        u_out[...] = (m_next * fix_one / (jnp.sqrt(v_next * fix_two) + 1e-08)).astype(jnp.bfloat16)

    def column(i, at):
        core = at[0] if kc == 0 else 1 - at[0]
        return (0, (core * 4 + (at[1] + 4 - kx) % 4) * 4 + (at[2] + 4 - i) % 4)

    block = pl.BlockSpec((rows, wide), column)
    ins = [
        pl.BlockSpec((wide, rank), lambda i, at: (i, 0)),
        pl.BlockSpec((rows, rank), lambda i, at: (0, 0)),
        block,
        block,
        block,
        block,
    ]
    args = [place, t, weight, grads, errors, moment, second]
    alias = {}
    if before is not None:
        ins += [pl.BlockSpec(memory_space=pl.ANY)] * 4
        alias = {len(args) + i: i for i in range(4)}
        args += list(before)
    return pl.pallas_call(
        body,
        grid_spec=pltpu.PrefetchScalarGridSpec(
            num_scalar_prefetch=1, grid=(4,), in_specs=ins, out_specs=[block] * 4
        ),
        out_shape=[
            jax.ShapeDtypeStruct((rows, cols), d) for d in (jnp.bfloat16, F32, F32, jnp.bfloat16)
        ],
        input_output_aliases=alias,
        compiler_params=params(),
        name="finish",
    )(*args)


def shift(value, axis, step):
    n = lax.axis_size(axis)
    return lax.ppermute(value, axis, [(i, (i + step) % n) for i in range(n)])


def device(y, x, core, z):
    return ((y * 4 + x) * 2 + core) * 8 + z


def spread(block, steps, held):
    pairs = []
    for y in range(4):
        for x in range(4):
            for core in range(2):
                for h in held:
                    z = (core * 4 + x + h) % 8
                    pairs.append((device(y, x, core, z), device(y, x, core, (z + steps) % 8)))
    return lax.ppermute(block, ALL, pairs)


def on_device(grads, errors, q_prev, moment, second):
    y, x, core, z = (lax.axis_index(a) for a in ALL)
    place = jnp.stack([core, x, y, z]).astype(jnp.int32)
    grads, errors = grads[0], errors[0]

    width = q_prev.shape[0] // 4
    away = (z - (core * 4 + x)) % 8
    right = lax.dynamic_slice_in_dim(q_prev, y * width, width, 0)
    held = [0]
    for step in (4, 2, 1):
        came = spread(right, step, held)
        new = [h + step for h in held]
        hit = functools.reduce(jnp.logical_or, [away == h for h in new])
        right = jnp.where(hit, came, right)
        held = held + new

    came = shift(add_half(place, grads, errors), "core", 1)
    pieces = add_pieces(place, grads, errors, came)
    pieces = [pieces[0]] + [shift(pieces[k], "x", k) for k in (1, 2, 3)]
    pieces = sum_split(place, pieces)
    pieces = [pieces[0]] + [shift(pieces[k], "y", k) for k in (1, 2, 3)]
    m, p = left_part(pieces, right)

    for axis in ("x", "y"):
        p = (p + shift(p, axis, 1)) + (shift(p, axis, 2) + shift(p, axis, 3))
    p = p + shift(p, "core", 1)

    mine = lax.all_to_all(products(m, p), "z", 0, 0)
    mine = jnp.sum(mine, axis=0)
    whole = lax.all_to_all(jnp.broadcast_to(mine, (8,) + mine.shape), "z", 0, 0)
    high = m.shape[1] // 8
    rank = p.shape[1]
    t = whole[:, :high].reshape(m.shape[1], rank)
    gram = whole[:, high:].reshape(rank, rank)

    t = jnp.concatenate([t] + [shift(t, "y", k) for k in (1, 2, 3)], axis=0)
    ts = [t] + [shift(t, "x", k) for k in (1, 2, 3)]

    low = jnp.linalg.cholesky(gram)
    inverse = lax.linalg.triangular_solve(low, jnp.eye(rank, dtype=F32), left_side=True, lower=True)
    p_hat = jnp.dot(p, inverse.T, precision=HI)
    weight = jnp.dot(p_hat, inverse, precision=HI) * (1.0 / REPS)

    out = None
    mine = jnp.zeros_like(t)
    for k in range(4):
        for c, piece in enumerate((ts[k], shift(ts[k], "core", 1))):
            out = finish(place, (c, k), piece, weight, grads, errors, moment, second, out)
            owner = (core ^ c) * 4 + (x + 4 - k) % 4
            mine = jnp.where(owner == z, piece, mine)
    mine = jnp.dot(mine, inverse.T, precision=HI) * (1.0 / REPS)
    mine = mine.reshape(4, width, rank)
    q_next = jnp.concatenate(
        [lax.dynamic_slice_in_dim(mine, (y - j) % 4, 1, 0)[0] for j in range(4)], axis=0
    )
    e_next, m_next, v_next, update = out
    return (e_next[None], q_next, m_next, v_next, update)


def solution(mesh):
    grid = Mesh(mesh.devices.reshape(4, 4, 2, 8), ALL)
    rep = ("y", "x", "core")
    return jax.shard_map(
        on_device,
        mesh=grid,
        in_specs=(P(rep, "z", None), P(rep, "z", None), P("z", None), P("z", None), P("z", None)),
        out_specs=(P(rep, "z", None), P("z", None), P("z", None), P("z", None), P("z", None)),
        check_vma=False,
    )
```

time: 580 us -> 192 us (0.33)
  waiting for transfers between devices: 503 us -> 35.5 us
  starting transfers between devices: 0.16 us -> 41.6 us
  Pallas kernels: 0 us -> 39.7 us
  matrix products: 32.8 us -> 1.46 us
  blocking collectives: 0 us -> 27.9 us
  between operations: 13.8 us -> 0.92 us
  local copies, waits for them, and re-layouts: 2.59 us -> 15.2 us
    psum x3 -> x0, waiting for transfers between devices: 441 us -> none  [the longest x1 271 us: on_device(): q_sum = lax.psum(jnp.dot(merged.T, p_hat, precision=hi), ('rep', 'shard'))]
    all_gather x1 -> x0, waiting for transfers between devices: 60.5 us -> none  [on_device(): q_full = lax.all_gather(q_prev, 'shard', axis=0, tiled=True)]
    ppermute x0 -> x27, starting transfers between devices: none -> 41.6 us  [the longest x24 34.1 us: shift(): return lax.ppermute(value, axis, [(i, (i + step) % n) for i in range(n)])]
    pallas_call x0 -> x13, Pallas kernels: none -> 39.7 us  [the longest x8 30.2 us: finish(): pl.pallas_call(body, grid_spec=pltpu.PrefetchScalarGridSpec(num_scalar_pr...]
    ppermute x0 -> x27, waiting for transfers between devices: none -> 35.5 us  [the longest x24 33.6 us: shift(): return lax.ppermute(value, axis, [(i, (i + step) % n) for i in range(n)])]
    dot_general x4 -> x3, matrix products: 31.8 us -> 1.22 us  [the longest x1 0.74 us: on_device(): mine = jnp.dot(mine, inverse.T, precision=HI) * (1.0 / REPS)]
    all_to_all x0 -> x2, blocking collectives: none -> 27.9 us  [the longest x1 16.6 us: on_device(): mine = lax.all_to_all(products(m, p), 'z', 0, 0)]
    unnamed x6 -> x26, local copies, waits for them, and re-layouts: 0.83 us -> 13.5 us
  transfers between devices with their start and end apart: 4 -> 27, of which waited for: 4 -> 16; matrix products, arithmetic and copies ran while one was open for 0% -> 16% of each run, Pallas kernels for 0% -> 9%
where the time goes in v1:
time: 192 us; the launch traced here: 191 us
  starting transfers between devices  41.6 us (22%)
  Pallas kernels  39.7 us (21%)
  waiting for transfers between devices  35.5 us (18%)
  other arithmetic  28.6 us (15%)
  blocking collectives  27.9 us (15%)
  local copies, waits for them, and re-layouts  15.2 us (8%)
    ppermute x24, starting transfers between devices, shift(): return lax.ppermute(value, axis, [(i, (i + step) % n) for i in range(n)])  34.1 us
    ppermute x24, waiting for transfers between devices, shift(): return lax.ppermute(value, axis, [(i, (i + step) % n) for i in range(n)])  33.6 us
    pallas_call x8, Pallas kernels, finish(): pl.pallas_call(body, grid_spec=pltpu.PrefetchScalarGridSpec(num_scalar_pr...  30.2 us
    all_to_all x1, blocking collectives, on_device(): mine = lax.all_to_all(products(m, p), 'z', 0, 0)  16.6 us
    unnamed x26, local copies, waits for them, and re-layouts  13.5 us
    another operation x3, other arithmetic, on_device(): low = jnp.linalg.cholesky(gram)  13.2 us
    another operation x2, other arithmetic, on_device(): lax.linalg.triangular_solve(low, jnp.eye(rank, dtype=F32), left_side=True...  11.9 us
    all_to_all x1, blocking collectives, on_device(): whole = lax.all_to_all(jnp.broadcast_to(mine, (8,) + mine.shape), 'z', 0, 0)  11.3 us
  transfers between devices with their start and end apart: 27, of which 16 were waited for; matrix products, arithmetic and copies ran while one was open for 16% of the time, Pallas kernels for 9%

profile of v1, /device:TPU:1, one launch (start us, length us, event | category | flops | bytes accessed | tf_op | source)
XLA Modules:
  0.0 190.8 jit_solution(7681834793318209195)
XLA Ops:
  3.9 2.6 %add_half.1 = f32[128,4096]{1,0:T(8,128)} custom-call(s32[4]{0:T(128)S(1)} %pad_add_fusion.at, bf16[128,8192]{1,0:T(8,128)(2,1)S(1)} %bitcast.33, bf16[128,8192]{1,0:T(8,128)(2,1)S(1)} %bitcast.46), custom_call_target="tpu_custom_call" | custom-call | tf_op jit(solution)/shard_map/add_half/pallas_call | solution.py:39
  6.5 3.2 %collective-permute-start = (f32[128,4096]{1,0:T(8,128)}, f32[128,4096]{1,0:T(8,128)}, u32[]{:S(2)}, u32[]{:S(2)}) collective-permute-start(f32[128,4096]{1,0:T(8,128)} %add_half.1), channel_id=1, source_target_pairs={{0,8},{8,0},{1,9},{9,1},{2,10},{10,2},{3,11},{11,3},{4,12},{12,4},... | collective-permute-start | bytes 6291464 | tf_op jit(solution)/shard_map/ppermute | solution.py:207
  12.0 1.9 collective-permute-done.refs_2_.refs_5_.refs_8_.refs_11_
  15.4 4.4 %add_pieces.1 = (f32[128,1024]{1,0:T(8,128)S(1)}, f32[128,1024]{1,0:T(8,128)}, f32[128,1024]{1,0:T(8,128)}, f32[128,1024]{1,0:T(8,128)}) custom-call(s32[4]{0:T(128)S(1)} %pad_add_fusion.at, bf16[128,8192]{1,0:T(8,128)(2,1)S(1)} %bitcast.34, bf16[128,8192]{1,0:T(8,128)(2,1)S(1)} %bitcast.47, ...), custom_call_target="tpu_custom_call" | custom-call | tf_op jit(solution)/shard_map/add_pieces/pallas_call | solution.py:73
  19.9 1.9 %collective-permute-start.2 = (f32[128,1024]{1,0:T(8,128)}, f32[128,1024]{1,0:T(8,128)}, u32[]{:S(2)}, u32[]{:S(2)}) collective-permute-start(f32[128,1024]{1,0:T(8,128)} %get-tuple-element.49), channel_id=1, source_target_pairs={{0,32},{16,48},{32,0},{48,16},{1,33},{17,49},{33,1},{49,17},{2,34}... | collective-permute-start | bytes 1572872 | tf_op jit(solution)/shard_map/ppermute | solution.py:207
  23.9 4.9 %collective-permute-start.8 = (f32[256,128]{1,0:T(8,128)S(1)}, f32[256,128]{1,0:T(8,128)S(1)}, u32[]{:S(2)}, u32[]{:S(2)}) collective-permute-start(f32[256,128]{1,0:T(8,128)S(1)} %broadcast_select_fusion), channel_id=1, source_target_pairs={{0,2},{4,6},{12,14},{8,10},{17,19},{21,23},{29,31},{25,27},{34,36}... | collective-permute-start | bytes 393224 | tf_op jit(solution)/shard_map/ppermute | solution.py:222
  28.8 1.9 %collective-permute-done.8 = f32[256,128]{1,0:T(8,128)S(1)} collective-permute-done((f32[256,128]{1,0:T(8,128)S(1)}, f32[256,128]{1,0:T(8,128)S(1)}, u32[]{:S(2)}, u32[]{:S(2)}) %collective-permute-start.8) | collective-permute-done | bytes 131104 | tf_op jit(solution)/shard_map/ppermute | solution.py:222
  32.1 13.0 %collective-permute-done.2.refs_2_ = f32[128,1024]{1,0:T(8,128)} collective-permute-done((f32[128,1024]{1,0:T(8,128)}, f32[128,1024]{1,0:T(8,128)}, u32[]{:S(2)}, u32[]{:S(2)}) %collective-permute-start.2) | collective-permute-done | bytes 524320 | tf_op jit(solution)/shard_map/ppermute | solution.py:207
  46.0 1.9 sum_split.1
  48.3 2.6 %collective-permute-start.5 = (f32[128,256]{1,0:T(8,128)S(1)}, f32[128,256]{1,0:T(8,128)S(1)}, u32[]{:S(2)}, u32[]{:S(2)}) collective-permute-start(f32[128,256]{1,0:T(8,128)S(1)} %get-tuple-element.53), channel_id=1, source_target_pairs={{0,128},{64,192},{128,0},{192,64},{1,129},{65,193},{129,1},{193,65... | collective-permute-start | bytes 393224 | tf_op jit(solution)/shard_map/ppermute | solution.py:207
  53.0 2.7 %collective-permute-done.5.c = f32[128,256]{1,0:T(8,128)S(1)} collective-permute-done((f32[128,256]{1,0:T(8,128)S(1)}, f32[128,256]{1,0:T(8,128)S(1)}, u32[]{:S(2)}, u32[]{:S(2)}) %collective-permute-start.5) | collective-permute-done | bytes 131104 | tf_op jit(solution)/shard_map/ppermute | solution.py:207
  56.0 4.7 %collective-permute-start.12 = (f32[128,128]{1,0:T(8,128)S(1)}, f32[128,128]{1,0:T(8,128)S(1)}, u32[]{:S(2)}, u32[]{:S(2)}) collective-permute-start(f32[128,128]{1,0:T(8,128)S(1)} %get-tuple-element.56), channel_id=1, source_target_pairs={{0,48},{16,0},{32,16},{48,32},{1,49},{17,1},{33,17},{49,33},{2,50}... | collective-permute-start | bytes 196616 | tf_op jit(solution)/shard_map/ppermute | solution.py:207
  62.0 3.4 %collective-permute-done.11 = f32[128,128]{1,0:T(8,128)S(1)} collective-permute-done((f32[128,128]{1,0:T(8,128)S(1)}, f32[128,128]{1,0:T(8,128)S(1)}, u32[]{:S(2)}, u32[]{:S(2)}) %collective-permute-start.11) | collective-permute-done | bytes 65568 | tf_op jit(solution)/shard_map/ppermute | solution.py:207
  65.8 2.9 %collective-permute-start.15 = (f32[128,128]{1,0:T(8,128)S(1)}, f32[128,128]{1,0:T(8,128)S(1)}, u32[]{:S(2)}, u32[]{:S(2)}) collective-permute-start(f32[128,128]{1,0:T(8,128)S(1)} %add_add_fusion.1), channel_id=1, source_target_pairs={{0,192},{64,0},{128,64},{192,128},{1,193},{65,1},{129,65},{193,129... | collective-permute-start | bytes 196616 | tf_op jit(solution)/shard_map/ppermute | solution.py:207
  70.0 3.4 %collective-permute-done.14 = f32[128,128]{1,0:T(8,128)S(1)} collective-permute-done((f32[128,128]{1,0:T(8,128)S(1)}, f32[128,128]{1,0:T(8,128)S(1)}, u32[]{:S(2)}, u32[]{:S(2)}) %collective-permute-start.14) | collective-permute-done | bytes 65568 | tf_op jit(solution)/shard_map/ppermute | solution.py:207
  73.7 4.1 %collective-permute-start.16 = (f32[128,128]{1,0:T(8,128)S(1)}, f32[128,128]{1,0:T(8,128)S(1)}, u32[]{:S(2)}, u32[]{:S(2)}) collective-permute-start(f32[128,128]{1,0:T(8,128)S(1)} %add_add_fusion), channel_id=1, source_target_pairs={{0,8},{8,0},{1,9},{9,1},{2,10},{10,2},{3,11},{11,3},{4,12},{12,4},... | collective-permute-start | bytes 196616 | tf_op jit(solution)/shard_map/ppermute | solution.py:207
  79.1 16.6 %all_to_all.10 = f32[8,48,128]{2,1,0:T(8,128)S(1)} all-to-all(f32[8,48,128]{2,1,0:T(8,128)S(1)} %products.1), channel_id=1, replica_groups=mesh['y'=4,'x'=4,'core'=2,'z'=8] {'z'}, dimensions={0} | all-to-all | bytes 393216 | tf_op jit(solution)/shard_map/all_to_all | solution.py:252
  95.7 11.3 %all_to_all.11 = f32[8,48,128]{2,1,0:T(8,128)S(1)} all-to-all(f32[8,48,128]{2,1,0:T(8,128)S(1)} %broadcast_in_dim.11), channel_id=1, replica_groups=mesh['y'=4,'x'=4,'core'=2,'z'=8] {'z'}, dimensions={0} | all-to-all | bytes 393216 | tf_op jit(solution)/shard_map/all_to_all | solution.py:254
  118.8 12.5 %cholesky.17 = f32[128,128]{1,0:T(8,128)S(1)} custom-call(f32[128,128]{1,0:T(8,128)} %fusion.20), custom_call_target="Cholesky" | custom-call | tf_op jit(solution)/shard_map/jit(cholesky)/cholesky | solution.py:263
  133.4 10.6 %custom-call.6 = f32[1,128,128]{1,2,0:T(8,128)S(1)} custom-call(f32[1,128,128]{2,1,0:T(8,128)} %fusion.17), custom_call_target="InvertDiagBlocksLowerTriangular" | custom-call | tf_op jit(solution)/shard_map/triangular_solve | solution.py:264
  144.0 5.2 %collective-permute-start.26 = (f32[1024,128]{1,0:T(8,128)S(1)}, f32[1024,128]{1,0:T(8,128)S(1)}, u32[]{:S(2)}, u32[]{:S(2)}) collective-permute-start(f32[1024,128]{1,0:T(8,128)S(1)} %pad_maximum_fusion.t_ref), channel_id=1, source_target_pairs={{0,8},{8,0},{1,9},{9,1},{2,10},{10,2},{3,11},{11,3},{4,12},{12,4},... | collective-permute-start | bytes 1572872 | tf_op jit(solution)/shard_map/ppermute | solution.py:207
  152.4 2.2 %copy-done.5 = f32[128,8192]{1,0:T(8,128)S(1)} copy-done((f32[128,8192]{1,0:T(8,128)S(1)}, f32[128,8192]{1,0:T(8,128)}, u32[]{:S(2)}) %copy-start.5) | copy-done | bytes 4194328
  154.6 2.2 %copy-done.7 = f32[128,8192]{1,0:T(8,128)S(1)} copy-done((f32[128,8192]{1,0:T(8,128)S(1)}, f32[128,8192]{1,0:T(8,128)}, u32[]{:S(2)}) %copy-start.7) | copy-done | bytes 4194328
  156.8 3.5 %finish.8 = (bf16[128,8192]{1,0:T(8,128)(2,1)}, f32[128,8192]{1,0:T(8,128)}, f32[128,8192]{1,0:T(8,128)}, bf16[128,8192]{1,0:T(8,128)(2,1)}) custom-call(s32[4]{0:T(128)S(1)} %pad_add_fusion.at, f32[1024,128]{1,0:T(8,128)S(1)} %pad_maximum_fusion.t_ref, f32[128,128]{1,0:T(8,128)S(1)} %convolution_multiply_fusion.1.w_ref, bf16[128,8192]{1,0:T(8,128)(2,1)S(1)} %bitcast.38, ...), custom_call_target="tpu_custom_call" | custom-call | tf_op jit(solution)/shard_map/finish/pallas_call | solution.py:191
  160.3 2.2 %copy-done.8 = f32[128,8192]{1,0:T(8,128)S(1)} copy-done((f32[128,8192]{1,0:T(8,128)S(1)}, f32[128,8192]{1,0:T(8,128)}, u32[]{:S(2)}) %copy-start.8) | copy-done | bytes 4194328
  162.5 3.5 %finish.9 = (bf16[128,8192]{1,0:T(8,128)(2,1)}, f32[128,8192]{1,0:T(8,128)}, f32[128,8192]{1,0:T(8,128)}, bf16[128,8192]{1,0:T(8,128)(2,1)}) custom-call(s32[4]{0:T(128)S(1)} %pad_add_fusion.at, f32[1024,128]{1,0:T(8,128)S(1)} %collective-permute-done.26.t_ref, ...), custom_call_target="tpu_custom_call", output_to_operand_aliasing={{0}: (7, {}), {1}: (8, {}), {2}: (9, {}), {3}: (10, {})} | custom-call | tf_op jit(solution)/shard_map/finish/pallas_call | solution.py:191
  166.0 4.6 %finish.10 = (bf16[128,8192]{1,0:T(8,128)(2,1)}, f32[128,8192]{1,0:T(8,128)}, f32[128,8192]{1,0:T(8,128)}, bf16[128,8192]{1,0:T(8,128)(2,1)}) custom-call(s32[4]{0:T(128)S(1)} %pad_add_fusion.at, f32[1024,128]{1,0:T(8,128)} %collective-permute-done.24.t_ref, ...), custom_call_target="tpu_custom_call", output_to_operand_aliasing={{0}: (7, {}), {1}: (8, {}), {2}: (9, {}), {3}: (10, {})} | custom-call | tf_op jit(solution)/shard_map/finish/pallas_call | solution.py:191
  172.2 3.5 %finish.11 = (bf16[128,8192]{1,0:T(8,128)(2,1)}, f32[128,8192]{1,0:T(8,128)}, f32[128,8192]{1,0:T(8,128)}, bf16[128,8192]{1,0:T(8,128)(2,1)}) custom-call(s32[4]{0:T(128)S(1)} %pad_add_fusion.at, f32[1024,128]{1,0:T(8,128)S(1)} %collective-permute-done.25.t_ref, ...), custom_call_target="tpu_custom_call", output_to_operand_aliasing={{0}: (7, {}), {1}: (8, {}), {2}: (9, {}), {3}: (10, {})} | custom-call | tf_op jit(solution)/shard_map/finish/pallas_call | solution.py:191
  175.7 4.6 %finish.12 = (bf16[128,8192]{1,0:T(8,128)(2,1)}, f32[128,8192]{1,0:T(8,128)}, f32[128,8192]{1,0:T(8,128)}, bf16[128,8192]{1,0:T(8,128)(2,1)}) custom-call(s32[4]{0:T(128)S(1)} %pad_add_fusion.at, f32[1024,128]{1,0:T(8,128)} %collective-permute-done.22.t_ref, ...), custom_call_target="tpu_custom_call", output_to_operand_aliasing={{0}: (7, {}), {1}: (8, {}), {2}: (9, {}), {3}: (10, {})} | custom-call | tf_op jit(solution)/shard_map/finish/pallas_call | solution.py:191
  180.3 3.5 %finish.13 = (bf16[128,8192]{1,0:T(8,128)(2,1)}, f32[128,8192]{1,0:T(8,128)}, f32[128,8192]{1,0:T(8,128)}, bf16[128,8192]{1,0:T(8,128)(2,1)}) custom-call(s32[4]{0:T(128)S(1)} %pad_add_fusion.at, f32[1024,128]{1,0:T(8,128)S(1)} %collective-permute-done.23.t_ref, ...), custom_call_target="tpu_custom_call", output_to_operand_aliasing={{0}: (7, {}), {1}: (8, {}), {2}: (9, {}), {3}: (10, {})} | custom-call | tf_op jit(solution)/shard_map/finish/pallas_call | solution.py:191
  183.8 3.5 %finish.14 = (bf16[128,8192]{1,0:T(8,128)(2,1)}, f32[128,8192]{1,0:T(8,128)}, f32[128,8192]{1,0:T(8,128)}, bf16[128,8192]{1,0:T(8,128)(2,1)}) custom-call(s32[4]{0:T(128)S(1)} %pad_add_fusion.at, f32[1024,128]{1,0:T(8,128)S(1)} %collective-permute-done.20.t_ref, ...), custom_call_target="tpu_custom_call", output_to_operand_aliasing={{0}: (7, {}), {1}: (8, {}), {2}: (9, {}), {3}: (10, {})} | custom-call | tf_op jit(solution)/shard_map/finish/pallas_call | solution.py:191
  187.3 3.5 %finish.15 = (bf16[128,8192]{1,0:T(8,128)(2,1)}, f32[128,8192]{1,0:T(8,128)}, f32[128,8192]{1,0:T(8,128)}, bf16[128,8192]{1,0:T(8,128)(2,1)}) custom-call(s32[4]{0:T(128)S(1)} %pad_add_fusion.at, f32[1024,128]{1,0:T(8,128)S(1)} %collective-permute-done.21.t_ref, ...), custom_call_target="tpu_custom_call", output_to_operand_aliasing={{0}: (7, {}), {1}: (8, {}), {2}: (9, {}), {3}: (10, {})} | custom-call | tf_op jit(solution)/shard_map/finish/pallas_call | solution.py:191
  (89 shorter events, 37.4 us)
Async XLA Ops:
  3.9 9.9 %copy-start.1 = (bf16[1,128,8192]{2,1,0:T(8,128)(2,1)S(1)}, bf16[1,128,8192]{2,1,0:T(8,128)(2,1)}, u32[]{:S(2)}) copy-start(bf16[1,128,8192]{2,1,0:T(8,128)(2,1)} %param.5) | copy-start | bytes 6291460
  6.5 7.4 %collective-permute-start = (f32[128,4096]{1,0:T(8,128)}, f32[128,4096]{1,0:T(8,128)}, u32[]{:S(2)}, u32[]{:S(2)}) collective-permute-start(f32[128,4096]{1,0:T(8,128)} %add_half.1), channel_id=1, source_target_pairs={{0,8},{8,0},{1,9},{9,1},{2,10},{10,2},{3,11},{11,3},{4,12},{12,4},... | collective-permute-start | bytes 6291464 | tf_op jit(solution)/shard_map/ppermute | solution.py:207
  10.6 12.3 %collective-permute-start.7 = (f32[256,128]{1,0:T(8,128)S(1)}, f32[256,128]{1,0:T(8,128)S(1)}, u32[]{:S(2)}, u32[]{:S(2)}) collective-permute-start(f32[256,128]{1,0:T(8,128)S(1)} %constant_dynamic-slice_fusion), channel_id=1, source_target_pairs={{0,4},{12,8},{17,21},{29,25},{34,38},{46,42},{51,55},{63,59},{64,6... | collective-permute-start | bytes 393224 | tf_op jit(solution)/shard_map/ppermute | solution.py:222
  19.9 12.2 %collective-permute-start.1 = (f32[128,1024]{1,0:T(8,128)}, f32[128,1024]{1,0:T(8,128)S(1)}, u32[]{:S(2)}, u32[]{:S(2)}) collective-permute-start(f32[128,1024]{1,0:T(8,128)} %get-tuple-element.48), channel_id=1, source_target_pairs={{0,16},{16,32},{32,48},{48,0},{1,17},{17,33},{33,49},{49,1},{2,18}... | collective-permute-start | bytes 1572872 | tf_op jit(solution)/shard_map/ppermute | solution.py:207
  19.9 25.2 %collective-permute-start.2 = (f32[128,1024]{1,0:T(8,128)}, f32[128,1024]{1,0:T(8,128)}, u32[]{:S(2)}, u32[]{:S(2)}) collective-permute-start(f32[128,1024]{1,0:T(8,128)} %get-tuple-element.49), channel_id=1, source_target_pairs={{0,32},{16,48},{32,0},{48,16},{1,33},{17,49},{33,1},{49,17},{2,34}... | collective-permute-start | bytes 1572872 | tf_op jit(solution)/shard_map/ppermute | solution.py:207
  21.8 24.2 %collective-permute-start.3 = (f32[128,1024]{1,0:T(8,128)}, f32[128,1024]{1,0:T(8,128)}, u32[]{:S(2)}, u32[]{:S(2)}) collective-permute-start(f32[128,1024]{1,0:T(8,128)} %get-tuple-element.50), channel_id=1, source_target_pairs={{0,48},{16,0},{32,16},{48,32},{1,49},{17,1},{33,17},{49,33},{2,50}... | collective-permute-start | bytes 1572872 | tf_op jit(solution)/shard_map/ppermute | solution.py:207
  23.9 6.8 %collective-permute-start.8 = (f32[256,128]{1,0:T(8,128)S(1)}, f32[256,128]{1,0:T(8,128)S(1)}, u32[]{:S(2)}, u32[]{:S(2)}) collective-permute-start(f32[256,128]{1,0:T(8,128)S(1)} %broadcast_select_fusion), channel_id=1, source_target_pairs={{0,2},{4,6},{12,14},{8,10},{17,19},{21,23},{29,31},{25,27},{34,36}... | collective-permute-start | bytes 393224 | tf_op jit(solution)/shard_map/ppermute | solution.py:222
  30.7 21.2 %collective-permute-start.9 = (f32[256,128]{1,0:T(8,128)S(1)}, f32[256,128]{1,0:T(8,128)S(1)}, u32[]{:S(2)}, u32[]{:S(2)}) collective-permute-start(f32[256,128]{1,0:T(8,128)S(1)} %broadcast_select_fusion.1), channel_id=1, source_target_pairs={{0,1},{4,5},{2,3},{6,7},{12,13},{8,9},{14,15},{10,11},{17,18},{21,... | collective-permute-start | bytes 393224 | tf_op jit(solution)/shard_map/ppermute | solution.py:222
  47.9 5.1 %collective-permute-start.4 = (f32[128,256]{1,0:T(8,128)S(1)}, f32[128,256]{1,0:T(8,128)S(1)}, u32[]{:S(2)}, u32[]{:S(2)}) collective-permute-start(f32[128,256]{1,0:T(8,128)S(1)} %get-tuple-element.52), channel_id=1, source_target_pairs={{0,64},{64,128},{128,192},{192,0},{1,65},{65,129},{129,193},{193,1... | collective-permute-start | bytes 393224 | tf_op jit(solution)/shard_map/ppermute | solution.py:207
  48.3 7.5 %collective-permute-start.5 = (f32[128,256]{1,0:T(8,128)S(1)}, f32[128,256]{1,0:T(8,128)S(1)}, u32[]{:S(2)}, u32[]{:S(2)}) collective-permute-start(f32[128,256]{1,0:T(8,128)S(1)} %get-tuple-element.53), channel_id=1, source_target_pairs={{0,128},{64,192},{128,0},{192,64},{1,129},{65,193},{129,1},{193,65... | collective-permute-start | bytes 393224 | tf_op jit(solution)/shard_map/ppermute | solution.py:207
  50.9 4.8 %collective-permute-start.6 = (f32[128,256]{1,0:T(8,128)S(1)}, f32[128,256]{1,0:T(8,128)S(1)}, u32[]{:S(2)}, u32[]{:S(2)}) collective-permute-start(f32[128,256]{1,0:T(8,128)S(1)} %get-tuple-element.54), channel_id=1, source_target_pairs={{0,192},{64,0},{128,64},{192,128},{1,193},{65,1},{129,65},{193,129... | collective-permute-start | bytes 393224 | tf_op jit(solution)/shard_map/ppermute | solution.py:207
  56.0 6.0 %collective-permute-start.12 = (f32[128,128]{1,0:T(8,128)S(1)}, f32[128,128]{1,0:T(8,128)S(1)}, u32[]{:S(2)}, u32[]{:S(2)}) collective-permute-start(f32[128,128]{1,0:T(8,128)S(1)} %get-tuple-element.56), channel_id=1, source_target_pairs={{0,48},{16,0},{32,16},{48,32},{1,49},{17,1},{33,17},{49,33},{2,50}... | collective-permute-start | bytes 196616 | tf_op jit(solution)/shard_map/ppermute | solution.py:207
  60.7 4.7 %collective-permute-start.11 = (f32[128,128]{1,0:T(8,128)S(1)}, f32[128,128]{1,0:T(8,128)S(1)}, u32[]{:S(2)}, u32[]{:S(2)}) collective-permute-start(f32[128,128]{1,0:T(8,128)S(1)} %get-tuple-element.56), channel_id=1, source_target_pairs={{0,32},{16,48},{32,0},{48,16},{1,33},{17,49},{33,1},{49,17},{2,34}... | collective-permute-start | bytes 196616 | tf_op jit(solution)/shard_map/ppermute | solution.py:207
  60.7 5.0 %collective-permute-start.10 = (f32[128,128]{1,0:T(8,128)S(1)}, f32[128,128]{1,0:T(8,128)S(1)}, u32[]{:S(2)}, u32[]{:S(2)}) collective-permute-start(f32[128,128]{1,0:T(8,128)S(1)} %get-tuple-element.56), channel_id=1, source_target_pairs={{0,16},{16,32},{32,48},{48,0},{1,17},{17,33},{33,49},{49,1},{2,18}... | collective-permute-start | bytes 196616 | tf_op jit(solution)/shard_map/ppermute | solution.py:207
  65.8 4.2 %collective-permute-start.15 = (f32[128,128]{1,0:T(8,128)S(1)}, f32[128,128]{1,0:T(8,128)S(1)}, u32[]{:S(2)}, u32[]{:S(2)}) collective-permute-start(f32[128,128]{1,0:T(8,128)S(1)} %add_add_fusion.1), channel_id=1, source_target_pairs={{0,192},{64,0},{128,64},{192,128},{1,193},{65,1},{129,65},{193,129... | collective-permute-start | bytes 196616 | tf_op jit(solution)/shard_map/ppermute | solution.py:207
  68.6 4.7 %collective-permute-start.14 = (f32[128,128]{1,0:T(8,128)S(1)}, f32[128,128]{1,0:T(8,128)S(1)}, u32[]{:S(2)}, u32[]{:S(2)}) collective-permute-start(f32[128,128]{1,0:T(8,128)S(1)} %add_add_fusion.1), channel_id=1, source_target_pairs={{0,128},{64,192},{128,0},{192,64},{1,129},{65,193},{129,1},{193,65... | collective-permute-start | bytes 196616 | tf_op jit(solution)/shard_map/ppermute | solution.py:207
  68.6 5.0 %collective-permute-start.13 = (f32[128,128]{1,0:T(8,128)S(1)}, f32[128,128]{1,0:T(8,128)S(1)}, u32[]{:S(2)}, u32[]{:S(2)}) collective-permute-start(f32[128,128]{1,0:T(8,128)S(1)} %add_add_fusion.1), channel_id=1, source_target_pairs={{0,64},{64,128},{128,192},{192,0},{1,65},{65,129},{129,193},{193,1... | collective-permute-start | bytes 196616 | tf_op jit(solution)/shard_map/ppermute | solution.py:207
  73.7 5.0 %collective-permute-start.16 = (f32[128,128]{1,0:T(8,128)S(1)}, f32[128,128]{1,0:T(8,128)S(1)}, u32[]{:S(2)}, u32[]{:S(2)}) collective-permute-start(f32[128,128]{1,0:T(8,128)S(1)} %add_add_fusion), channel_id=1, source_target_pairs={{0,8},{8,0},{1,9},{9,1},{2,10},{10,2},{3,11},{11,3},{4,12},{12,4},... | collective-permute-start | bytes 196616 | tf_op jit(solution)/shard_map/ppermute | solution.py:207
  107.0 4.1 %collective-permute-start.19 = (f32[256,128]{1,0:T(8,128)S(1)}, f32[256,128]{1,0:T(8,128)S(1)}, u32[]{:S(2)}, u32[]{:S(2)}) collective-permute-start(f32[256,128]{1,0:T(8,128)S(1)} %bitcast.61), channel_id=1, source_target_pairs={{0,192},{64,0},{128,64},{192,128},{1,193},{65,1},{129,65},{193,129... | collective-permute-start | bytes 393224 | tf_op jit(solution)/shard_map/ppermute | solution.py:207
  107.4 5.4 %collective-permute-start.18 = (f32[256,128]{1,0:T(8,128)S(1)}, f32[256,128]{1,0:T(8,128)S(1)}, u32[]{:S(2)}, u32[]{:S(2)}) collective-permute-start(f32[256,128]{1,0:T(8,128)S(1)} %bitcast.62), channel_id=1, source_target_pairs={{0,128},{64,192},{128,0},{192,64},{1,129},{65,193},{129,1},{193,65... | collective-permute-start | bytes 393224 | tf_op jit(solution)/shard_map/ppermute | solution.py:207
  108.3 5.9 %collective-permute-start.17 = (f32[256,128]{1,0:T(8,128)S(1)}, f32[256,128]{1,0:T(8,128)S(1)}, u32[]{:S(2)}, u32[]{:S(2)}) collective-permute-start(f32[256,128]{1,0:T(8,128)S(1)} %bitcast.63), channel_id=1, source_target_pairs={{0,64},{64,128},{128,192},{192,0},{1,65},{65,129},{129,193},{193,1... | collective-permute-start | bytes 393224 | tf_op jit(solution)/shard_map/ppermute | solution.py:207
  114.2 35.1 %collective-permute-start.24 = (f32[1024,128]{1,0:T(8,128)S(1)}, f32[1024,128]{1,0:T(8,128)}, u32[]{:S(2)}, u32[]{:S(2)}) collective-permute-start(f32[1024,128]{1,0:T(8,128)S(1)} %pad_maximum_fusion.t_ref), channel_id=1, source_target_pairs={{0,16},{16,32},{32,48},{48,0},{1,17},{17,33},{33,49},{49,1},{2,18}... | collective-permute-start | bytes 1572872 | tf_op jit(solution)/shard_map/ppermute | solution.py:207
  114.8 34.5 %collective-permute-start.22 = (f32[1024,128]{1,0:T(8,128)S(1)}, f32[1024,128]{1,0:T(8,128)}, u32[]{:S(2)}, u32[]{:S(2)}) collective-permute-start(f32[1024,128]{1,0:T(8,128)S(1)} %pad_maximum_fusion.t_ref), channel_id=1, source_target_pairs={{0,32},{16,48},{32,0},{48,16},{1,33},{17,49},{33,1},{49,17},{2,34}... | collective-permute-start | bytes 1572872 | tf_op jit(solution)/shard_map/ppermute | solution.py:207
  115.8 33.9 %collective-permute-start.20 = (f32[1024,128]{1,0:T(8,128)S(1)}, f32[1024,128]{1,0:T(8,128)S(1)}, u32[]{:S(2)}, u32[]{:S(2)}) collective-permute-start(f32[1024,128]{1,0:T(8,128)S(1)} %pad_maximum_fusion.t_ref), channel_id=1, source_target_pairs={{0,48},{16,0},{32,16},{48,32},{1,49},{17,1},{33,17},{49,33},{2,50}... | collective-permute-start | bytes 1572872 | tf_op jit(solution)/shard_map/ppermute | solution.py:207
  144.0 16.3 %collective-permute-start.26 = (f32[1024,128]{1,0:T(8,128)S(1)}, f32[1024,128]{1,0:T(8,128)S(1)}, u32[]{:S(2)}, u32[]{:S(2)}) collective-permute-start(f32[1024,128]{1,0:T(8,128)S(1)} %pad_maximum_fusion.t_ref), channel_id=1, source_target_pairs={{0,8},{8,0},{1,9},{9,1},{2,10},{10,2},{3,11},{11,3},{4,12},{12,4},... | collective-permute-start | bytes 1572872 | tf_op jit(solution)/shard_map/ppermute | solution.py:207
  149.2 21.3 %collective-permute-start.25 = (f32[1024,128]{1,0:T(8,128)}, f32[1024,128]{1,0:T(8,128)S(1)}, u32[]{:S(2)}, u32[]{:S(2)}) collective-permute-start(f32[1024,128]{1,0:T(8,128)} %collective-permute-done.24.t_ref), channel_id=1, source_target_pairs={{0,8},{8,0},{1,9},{9,1},{2,10},{10,2},{3,11},{11,3},{4,12},{12,4},... | collective-permute-start | bytes 1572872 | tf_op jit(solution)/shard_map/ppermute | solution.py:207
  149.3 21.2 %collective-permute-start.23 = (f32[1024,128]{1,0:T(8,128)}, f32[1024,128]{1,0:T(8,128)S(1)}, u32[]{:S(2)}, u32[]{:S(2)}) collective-permute-start(f32[1024,128]{1,0:T(8,128)} %collective-permute-done.22.t_ref), channel_id=1, source_target_pairs={{0,8},{8,0},{1,9},{9,1},{2,10},{10,2},{3,11},{11,3},{4,12},{12,4},... | collective-permute-start | bytes 1572872 | tf_op jit(solution)/shard_map/ppermute | solution.py:207
  149.7 20.8 %collective-permute-start.21 = (f32[1024,128]{1,0:T(8,128)S(1)}, f32[1024,128]{1,0:T(8,128)S(1)}, u32[]{:S(2)}, u32[]{:S(2)}) collective-permute-start(f32[1024,128]{1,0:T(8,128)S(1)} %collective-permute-done.20.t_ref), channel_id=1, source_target_pairs={{0,8},{8,0},{1,9},{9,1},{2,10},{10,2},{3,11},{11,3},{4,12},{12,4},... | collective-permute-start | bytes 1572872 | tf_op jit(solution)/shard_map/ppermute | solution.py:207
  156.8 3.5 %copy-start.6 = (f32[128,8192]{1,0:T(8,128)S(1)}, f32[128,8192]{1,0:T(8,128)}, u32[]{:S(2)}) copy-start(f32[128,8192]{1,0:T(8,128)} %m.15) | copy-start | bytes 12582916
  160.3 2.2 %copy-start.8 = (f32[128,8192]{1,0:T(8,128)S(1)}, f32[128,8192]{1,0:T(8,128)}, u32[]{:S(2)}) copy-start(f32[128,8192]{1,0:T(8,128)} %v.15) | copy-start | bytes 12582916
  166.0 4.6 %copy-start.10 = (f32[256,128]{1,0:T(8,128)S(1)}, f32[256,128]{1,0:T(8,128)}, u32[]{:S(2)}) copy-start(f32[256,128]{1,0:T(8,128)} %copy-done.9) | copy-start | bytes 393220
  166.0 4.6 %copy-start.12 = (f32[256,128]{1,0:T(8,128)S(1)}, f32[256,128]{1,0:T(8,128)}, u32[]{:S(2)}) copy-start(f32[256,128]{1,0:T(8,128)} %copy-done.11) | copy-start | bytes 393220
  (8 other events, 12.9 us)
